TPU v7x, 32 devices: a whole 2x2x4 slice. The times are simulated.
32 devices in a mesh: seq: 4 (over z), grp: 8 (over y, x, core).
Axes of the slice: x: 2, y: 2, z: 4, core: 2. Of those that a mesh axis runs over, the one named last changes fastest.
Arguments:
- qkv: bfloat16 [8192, 3, 2048], P(('seq', 'grp')), may hold values from -6 to 6
- cluster_lists: int32 [16, 8, 1024], P('seq', 'grp'), may hold values from 0 to 8191, as said below
- w_out: bfloat16 [2048, 2048], replicated, may hold values from -0.125 to 0.125
- norm_gain: bfloat16 [2048], replicated, may hold values from 0.099609375 to 1.8984375
- router: bfloat16 [2048, 32], replicated, may hold values from -0.125 to 0.125
- expert_lists: int32 [32, 512], replicated, may hold values from 0 to 8191, as said below
- w_gate: bfloat16 [32, 2048, 768], P(('seq', 'grp')), may hold values from -0.125 to 0.125
- w_up: bfloat16 [32, 2048, 768], P(('seq', 'grp')), may hold values from -0.125 to 0.125
- w_down: bfloat16 [32, 768, 2048], P(('seq', 'grp')), may hold values from -0.21875 to 0.21875
Outputs:
- layer_out: bfloat16 [8192, 2048], P(('seq', 'grp'))
Inputs may be any that keep to these rules, and one draw needn't show every extreme that they name: `cluster_lists`: within each head the 8 lists are disjoint, each ascending, and together hold every one of the 8192 tokens once. Of the 256 tokens of an aligned block, one list holds at most 48, and for every head some list holds exactly 48. `expert_lists`: each list is ascending with distinct rows. Of the 256 rows of an aligned block, one list holds at most 24, and some list holds exactly 24.
All inputs are finite; a program needn't handle non-finite values.
Results may differ from a plain program's by a relative error of at most 0.019.
Values may be sent and summed in bfloat16 or wider, within the bound.
A program may use at most 128 MiB of HBM per device.

v0:
```python
import jax
import jax.numpy as jnp
from jax import lax
from jax.sharding import PartitionSpec as P


def for_sending(array):
    return jax.tree.map(lambda a: a.astype(jnp.bfloat16) if a.dtype == jnp.float32 else a, array)


def attend_slots(packed, token_at, key_valid, block_rows, score_scale):
    count_rows = packed.shape[0]
    queries = packed[:, 0, :]
    keys_all = packed[:, 1, :]
    values_all = packed[:, 2, :]
    pieces = []
    for row_start in range(0, count_rows, block_rows):
        row_end = min(row_start + block_rows, count_rows)
        scores = (
            jnp.einsum(
                "qd,kd->qk",
                queries[row_start:row_end],
                keys_all[:row_end],
                preferred_element_type=jnp.float32,
            )
            * score_scale
        )
        allowed = (token_at[row_start:row_end][:, None] >= token_at[:row_end][None, :]) & key_valid[
            :row_end
        ][None, :]
        scores = jnp.where(allowed, scores, -1e30)
        top_score = jnp.max(scores, axis=1, keepdims=True)
        exp_scores = jnp.exp(scores - top_score)
        weights = exp_scores.astype(jnp.bfloat16)
        totals = jnp.sum(exp_scores, axis=1, keepdims=True)
        summed = jnp.dot(weights, values_all[:row_end], preferred_element_type=jnp.float32)
        pieces.append((summed / totals).astype(jnp.bfloat16))
    return jnp.concatenate(pieces, axis=0)


def expert_mlp(rows_in, gate_w, up_w, down_w):
    gate_part = jnp.dot(rows_in, gate_w, preferred_element_type=jnp.float32)
    up_part = jnp.dot(rows_in, up_w, preferred_element_type=jnp.float32)
    hidden = (jax.nn.silu(gate_part) * up_part).astype(jnp.bfloat16)
    return jnp.dot(hidden, down_w, preferred_element_type=jnp.float32).astype(jnp.bfloat16)


def shards(qkv, cluster_lists, w_out, norm_gain, router, expert_lists, w_gate, w_up, w_down):
    local_rows = qkv.shape[0]
    seq_count = lax.axis_size("seq")
    grp_count = lax.axis_size("grp")
    device_count = seq_count * grp_count
    head_local = cluster_lists.shape[0]
    cluster_len = cluster_lists.shape[2]
    head_width = qkv.shape[2] // (head_local * seq_count)
    my_index = lax.axis_index("seq") * grp_count + lax.axis_index("grp")
    slot_cap = 3 * (local_rows // grp_count) // 2
    row_iota = jnp.arange(local_rows, dtype=jnp.int32)
    members = cluster_lists[:, 0, :]
    edges = jnp.arange(device_count + 1, dtype=jnp.int32) * local_rows
    starts_all = jnp.sum((members[:, None, :] < edges[None, :, None]).astype(jnp.int32), axis=2)
    first_pos = starts_all[:, :-1]
    counts = starts_all[:, 1:] - first_pos
    slots = jnp.arange(slot_cap, dtype=jnp.int32)
    positions = jnp.minimum(first_pos[:, :, None] + slots, cluster_len - 1)
    head_range = jnp.arange(head_local, dtype=jnp.int32)
    wanted = members[head_range[:, None, None], positions]
    slot_valid = slots < counts[:, :, None]
    request = jnp.where(slot_valid, wanted - edges[:-1][None, :, None], local_rows)
    asked = lax.all_to_all(request, ("seq", "grp"), split_axis=1, concat_axis=1, tiled=True)
    asked_grid = asked.reshape(head_local, seq_count, grp_count, slot_cap)
    selector = (asked_grid[..., None] == row_iota).astype(jnp.bfloat16)
    split_heads = qkv.reshape(local_rows, 3, seq_count, head_local, head_width)
    picked = jnp.einsum(
        "hsgcr,rkshd->hsgckd", selector, split_heads, preferred_element_type=jnp.float32
    ).astype(jnp.bfloat16)
    arrived = lax.all_to_all(
        picked.reshape(head_local, device_count, slot_cap, 3, head_width),
        ("seq", "grp"),
        split_axis=1,
        concat_axis=1,
        tiled=True,
    )
    arrived = arrived.reshape(head_local, device_count * slot_cap, 3, head_width)
    big_token = edges[-1]
    token_at = jnp.where(slot_valid, wanted, big_token).reshape(head_local, -1)
    key_valid = slot_valid.reshape(head_local, -1)
    block_rows = 512
    score_scale = head_width ** (-0.5)
    outputs = jax.vmap(
        lambda packed, tok, valid: attend_slots(packed, tok, valid, block_rows, score_scale)
    )(arrived, token_at, key_valid)
    returning = outputs.reshape(head_local, device_count, slot_cap, head_width)
    came_back = lax.all_to_all(
        for_sending(returning), ("seq", "grp"), split_axis=1, concat_axis=1, tiled=True
    ).astype(returning.dtype)
    came_grid = came_back.reshape(head_local, seq_count, grp_count, slot_cap, head_width)
    attended = jnp.einsum(
        "hsgcr,hsgcd->rshd", selector, came_grid, preferred_element_type=jnp.float32
    ).astype(jnp.bfloat16)
    mixed = jnp.dot(
        attended.reshape(local_rows, -1), w_out, preferred_element_type=jnp.float32
    ).astype(jnp.bfloat16)
    wide = mixed.astype(jnp.float32)
    mean_square = jnp.mean(wide * wide, axis=1, keepdims=True)
    normed = (wide * lax.rsqrt(mean_square + 1e-06) * norm_gain.astype(jnp.float32)).astype(
        jnp.bfloat16
    )
    gates = jax.nn.sigmoid(jnp.dot(normed, router, preferred_element_type=jnp.float32))
    expert_count = expert_lists.shape[0]
    chosen_len = expert_lists.shape[1]
    expert_cap = 3 * (chosen_len // device_count) // 2
    expert_starts = jnp.sum(
        (expert_lists[:, None, :] < edges[None, :, None]).astype(jnp.int32), axis=2
    )
    send_first = lax.dynamic_index_in_dim(expert_starts, my_index, 1, False)
    send_count = lax.dynamic_index_in_dim(expert_starts, my_index + 1, 1, False) - send_first
    expert_slots = jnp.arange(expert_cap, dtype=jnp.int32)
    expert_range = jnp.arange(expert_count, dtype=jnp.int32)[:, None]
    send_pos = jnp.minimum(send_first[:, None] + expert_slots, chosen_len - 1)
    send_rows = jnp.where(
        expert_slots < send_count[:, None],
        expert_lists[expert_range, send_pos] - my_index * local_rows,
        local_rows,
    )
    send_match = send_rows[..., None] == row_iota
    outgoing = jnp.einsum(
        "ecr,rd->ecd", send_match.astype(jnp.bfloat16), normed, preferred_element_type=jnp.float32
    ).astype(jnp.bfloat16)
    incoming = lax.all_to_all(outgoing, ("seq", "grp"), split_axis=0, concat_axis=0, tiled=True)
    flat_in = incoming.reshape(device_count * expert_cap, -1)
    outgoing_back = expert_mlp(flat_in, w_gate[0], w_up[0], w_down[0]).reshape(
        device_count, expert_cap, -1
    )
    results = lax.all_to_all(outgoing_back, ("seq", "grp"), split_axis=0, concat_axis=0, tiled=True)
    match_wide = send_match.astype(jnp.float32)
    weights = jnp.einsum("ecr,re->ec", match_wide, gates, precision=lax.Precision.HIGHEST)
    terms = weights[:, :, None] * results.astype(jnp.float32)
    combined = jnp.einsum("ecr,ecd->rd", match_wide, terms, precision=lax.Precision.HIGHEST)
    return (wide + combined).astype(jnp.bfloat16)


def solution(mesh):
    return jax.shard_map(
        shards,
        mesh=mesh,
        in_specs=(
            P(("seq", "grp"), None, None),
            P("seq", "grp", None),
            P(),
            P(),
            P(),
            P(),
            P(("seq", "grp"), None, None),
            P(("seq", "grp"), None, None),
            P(("seq", "grp"), None, None),
        ),
        out_specs=P(("seq", "grp"), None),
        check_vma=False,
    )
```

profile of v0, /device:TPU:0, one launch (start us, length us, event | category | flops | bytes accessed | tf_op | source)
XLA Modules:
  0.0 459.2 jit_solution(16318531125281441181)
XLA Ops:
  0.0 0.9 copy.110
  0.9 0.7 convert_reduce_fusion.1
  1.6 0.1 copy.54
  1.7 0.1 fusion.80
  1.8 0.1 reshape.196
  1.9 52.1 %gather_fusion = s32[6144]{0:T(1024)S(1)} fusion(s32[4,1024]{1,0:T(4,128)S(1)} %bitcast.81, s32[6144]{0:T(1024)S(1)} %reshape.196), kind=kCustom, calls=%fused_computation | custom fusion | bytes 98304 | tf_op jit(solution)/shard_map/gather | solution.py:67
  54.0 0.1 reshape.199
  54.1 0.1 copy.53
  54.2 0.1 subtract_select_fusion
  54.3 0.7 reshape.218
  55.1 7.3 %all-to-all-start = ((s32[32,1,192]{2,1,0:T(1,128)}), s32[32,1,192]{2,1,0:T(1,128)S(1)}, u32[]{:S(2)}, u32[]{:S(2)}) async-start(s32[32,1,192]{2,1,0:T(1,128)} %reshape.218), calls=%async_computation | async-start | bytes 65536 | tf_op jit(solution)/shard_map/all_to_all | solution.py:70
  62.4 6.1 %reshape.188 = bf16[256,3,4,4,128]{4,3,2,0,1:T(4,128)(2,1)} reshape(bf16[256,3,2048]{2,0,1:T(8,128)(2,1)} %param.9) | data formatting | bytes 6291456 | tf_op jit(solution)/shard_map/reshape | solution.py:73
  68.5 1.2 all-to-all-done
  69.6 0.5 broadcast.199
  70.2 0.7 reduce
  70.9 0.1 reshape.219
  71.0 3.8 fusion.26
  74.8 3.6 copy.60
  78.3 5.3 %all-to-all-start.1 = ((bf16[4,32,48,3,128]{4,2,3,0,1:T(8,128)(2,1)}), bf16[4,32,48,3,128]{4,2,3,0,1:T(8,128)(2,1)}, u32[]{:S(2)}, u32[]{:S(2)}) async-start(bf16[4,32,48,3,128]{4,2,3,0,1:T(8,128)(2,1)} %copy.60), calls=%async_computation.1 | async-start | bytes 9437184 | tf_op jit(solution)/shard_map/all_to_all | solution.py:77
  83.7 0.6 slice.63
  84.2 0.1 lt.124
  84.3 0.1 lt.125
  84.4 0.1 lt.118
  84.5 0.7 broadcast_select_fusion
  85.2 103.7 %all-to-all-done.1 = bf16[4,32,48,3,128]{4,2,3,0,1:T(8,128)(2,1)} async-done(((bf16[4,32,48,3,128]{4,2,3,0,1:T(8,128)(2,1)}), bf16[4,32,48,3,128]{4,2,3,0,1:T(8,128)(2,1)}, u32[]{:S(2)}, u32[]{:S(2)}) %all-to-all-start.1) | async-done | bytes 4718624 | tf_op jit(solution)/shard_map/all_to_all | solution.py:77
  188.9 3.4 copy.61
  192.4 0.3 slice_bitcast_fusion.1
  192.7 1.6 fusion.39
  194.3 1.6 fusion.17
  195.9 2.9 divide_convert_fusion.2
  198.8 2.9 fusion.13
  201.7 3.3 fusion.2
  205.0 3.5 divide_convert_fusion.1
  208.5 6.5 %fusion.93 = (f32[4,512]{1,0:T(4,128)S(1)}, f32[4,512,1536]{2,1,0:T(8,128)}) fusion(bf16[4,1536,3,128]{3,1,0,2:T(8,128)(2,1)S(1)} %bitcast.83, bf16[4,1536,128]{2,1,0:T(8,128)(2,1)S(1)} %get-tuple-element.9, pred[4,1536]{1,0:T(4,128)(4,1)S(1)} %get-tuple-element.6, s32[4,1536]{1,0:T(4,128)S(1)} %get-tuple-element.5, s32[4,512]{1,0:T(4,128)S(1)} %get-tuple-element.11), kind=kOutput, calls=%fused_computation.109 | convolution fusion | flops 821032960 | bytes 14727168 | tf_op jit(solution)/shard_map/vmap(qd,kd->qk)/dot_general | solution.py:20
  215.0 6.4 %fusion = f32[4,512]{1,0:T(4,128)S(1)} fusion(f32[4,512,1536]{2,1,0:T(8,128)} %get-tuple-element.18, f32[4,512]{1,0:T(4,128)S(1)} %get-tuple-element.17), kind=kLoop, calls=%fused_computation.4 | loop fusion | flops 6289408 | bytes 12599296 | tf_op jit(solution)/shard_map/vmap()/reduce_sum | solution.py:35
  221.3 6.6 %divide_convert_fusion = bf16[4,512,128]{2,1,0:T(8,128)(2,1)S(1)} fusion(f32[4,512,1536]{2,1,0:T(8,128)} %get-tuple-element.18, f32[4,512]{1,0:T(4,128)S(1)} %get-tuple-element.17, f32[4,512]{1,0:T(4,128)S(1)} %fusion, bf16[4,1536,3,128]{3,1,0,2:T(8,128)(2,1)S(1)} %bitcast.84), kind=kOutput, calls=%fused_computation.66 | convolution fusion | flops 812122112 | bytes 14696448 | tf_op jit(solution)/shard_map/vmap()/dot_general | solution.py:36
  227.9 0.1 pad_maximum_fusion
  228.1 0.0 copy-start.5
  228.1 0.0 copy-start.1
  228.1 1.3 copy.63
  229.4 3.9 all-to-all-start.2
  233.4 0.7 convert_reduce_fusion
  234.1 0.1 fusion.84
  234.2 0.1 reshape.202
  234.3 6.3 %gather_fusion.1 = s32[768]{0:T(1024)S(1)} fusion(s32[32,512]{1,0:T(8,128)S(1)} %copy-done.1, s32[768]{0:T(1024)S(1)} %reshape.202), kind=kCustom, calls=%fused_computation.1 | custom fusion | bytes 12288 | tf_op jit(solution)/shard_map/gather | solution.py:123
  240.6 0.1 reshape.210
  240.7 0.1 fusion.85
  240.8 0.1 copy.66
  240.8 0.2 iota_compare_fusion.4
  241.0 30.0 %all-to-all-done.2 = bf16[4,32,48,128]{3,2,0,1:T(8,128)(2,1)} async-done(((bf16[4,32,48,128]{3,2,0,1:T(8,128)(2,1)}), bf16[4,32,48,128]{3,2,0,1:T(8,128)(2,1)}, u32[]{:S(2)}, u32[]{:S(2)}) %all-to-all-start.2) | async-done | bytes 1572896 | tf_op jit(solution)/shard_map/all_to_all | solution.py:94
  271.1 3.2 bitcast_convert_fusion
  274.2 5.8 %fusion.40 = (f32[256]{0:T(256)S(1)}, bf16[256,2048]{1,0:T(8,128)(2,1)S(1)}) fusion(bf16[256,2048]{0,1:T(8,128)(2,1)S(1)} %bitcast.91, bf16[2048,2048]{1,0:T(8,128)(2,1)} %param.11), kind=kOutput, calls=%fused_computation.46 | convolution fusion | flops 2149580544 | bytes 10486784 | tf_op jit(solution)/shard_map/dot_general | solution.py:101
  280.1 1.1 convolution_convert_fusion.1
  281.2 0.0 copy-start.6
  281.2 75.0 %all_to_all.25 = bf16[32,24,2048]{2,1,0:T(8,128)(2,1)S(1)} all-to-all(bf16[32,24,2048]{2,1,0:T(8,128)(2,1)S(1)} %convolution_convert_fusion.1), channel_id=1, replica_groups=mesh['seq'=4,'grp'=8] {'seq','grp'}, dimensions={0} | all-to-all | bytes 6291456 | tf_op jit(solution)/shard_map/all_to_all | solution.py:130
  356.2 1.7 copy-done.4
  357.9 4.0 fusion.20
  361.9 11.0 %convolution_convert_fusion = bf16[768,2048]{1,0:T(8,128)(2,1)} fusion(bf16[1,768,2048]{2,1,0:T(8,128)(2,1)S(1)} %copy-done, f32[768,768]{1,0:T(8,128)} %fusion.20, bf16[768,2048]{1,0:T(8,128)(2,1)} %bitcast.90, bf16[1,2048,768]{2,1,0:T(8,128)(2,1)} %param.15), kind=kOutput, calls=%fused_computation.27 | convolution fusion | flops 4836950016 | bytes 14942208 | tf_op jit(solution)/shard_map/dot_general | solution.py:45
  372.9 4.0 all-to-all-start.4
  377.0 1.7 fusion.52
  378.7 0.5 fusion.67
  379.3 69.2 %all-to-all-done.4 = bf16[32,24,2048]{2,1,0:T(8,128)(2,1)} async-done(((bf16[32,24,2048]{2,1,0:T(8,128)(2,1)}), bf16[32,24,2048]{2,1,0:T(8,128)(2,1)}, u32[]{:S(2)}, u32[]{:S(2)}) %all-to-all-start.4) | async-done | bytes 3145760 | tf_op jit(solution)/shard_map/all_to_all | solution.py:135
  448.4 2.5 convert_multiply_fusion
  450.9 8.0 %fusion.36 = bf16[256,2048]{1,0:T(8,128)(2,1)} fusion(f32[32,24,2048]{2,1,0:T(8,128)S(1)} %convert_multiply_fusion, bf16[256,2048]{1,0:T(8,128)(2,1)S(1)} %copy-done.3, s32[32,24]{0,1:T(8,128)S(1)} %copy.66), kind=kOutput, calls=%fused_computation.41 | convolution fusion | flops 4833607680 | bytes 8391680 | tf_op jit(solution)/shard_map/ecr,ecd->rd/dot_general | solution.py:139
  (24 shorter events, 0.1 us)
Async XLA Ops:
  0.0 361.9 %copy-start = (bf16[1,768,2048]{2,1,0:T(8,128)(2,1)S(1)}, bf16[1,768,2048]{2,1,0:T(8,128)(2,1)}, u32[]{:S(2)}) copy-start(bf16[1,768,2048]{2,1,0:T(8,128)(2,1)} %param.17) | copy-start | bytes 9437188
  55.1 14.6 %all-to-all-start = ((s32[32,1,192]{2,1,0:T(1,128)}), s32[32,1,192]{2,1,0:T(1,128)S(1)}, u32[]{:S(2)}, u32[]{:S(2)}) async-start(s32[32,1,192]{2,1,0:T(1,128)} %reshape.218), calls=%async_computation | async-start | bytes 65536 | tf_op jit(solution)/shard_map/all_to_all | solution.py:70
  78.3 110.6 %all-to-all-start.1 = ((bf16[4,32,48,3,128]{4,2,3,0,1:T(8,128)(2,1)}), bf16[4,32,48,3,128]{4,2,3,0,1:T(8,128)(2,1)}, u32[]{:S(2)}, u32[]{:S(2)}) async-start(bf16[4,32,48,3,128]{4,2,3,0,1:T(8,128)(2,1)} %copy.60), calls=%async_computation.1 | async-start | bytes 9437184 | tf_op jit(solution)/shard_map/all_to_all | solution.py:77
  228.1 5.3 %copy-start.5 = (bf16[2048]{0:T(1024)(128)(2,1)S(1)}, bf16[2048]{0:T(1024)(128)(2,1)}, u32[]{:S(2)}) copy-start(bf16[2048]{0:T(1024)(128)(2,1)} %param.12) | copy-start | bytes 12292
  228.1 5.3 %copy-start.1 = (s32[32,512]{1,0:T(8,128)S(1)}, s32[32,512]{1,0:T(8,128)}, u32[]{:S(2)}) copy-start(s32[32,512]{1,0:T(8,128)} %param.14) | copy-start | bytes 196612
  229.4 41.6 %all-to-all-start.2 = ((bf16[4,32,48,128]{3,2,0,1:T(8,128)(2,1)}), bf16[4,32,48,128]{3,2,0,1:T(8,128)(2,1)}, u32[]{:S(2)}, u32[]{:S(2)}) async-start(bf16[4,32,48,128]{3,2,0,1:T(8,128)(2,1)} %copy.63), calls=%async_computation.2 | async-start | bytes 3145728 | tf_op jit(solution)/shard_map/all_to_all | solution.py:94
  280.0 76.2 %copy-start.2 = (bf16[256,2048]{1,0:T(8,128)(2,1)}, bf16[256,2048]{1,0:T(8,128)(2,1)S(1)}, u32[]{:S(2)}) copy-start(bf16[256,2048]{1,0:T(8,128)(2,1)S(1)} %get-tuple-element.24) | copy-start | bytes 3145732
  281.2 76.7 %copy-start.6 = (bf16[1,2048,768]{2,1,0:T(8,128)(2,1)S(1)}, bf16[1,2048,768]{2,1,0:T(8,128)(2,1)}, u32[]{:S(2)}) copy-start(bf16[1,2048,768]{2,1,0:T(8,128)(2,1)} %param.16) | copy-start | bytes 9437188
  356.2 1.7 copy-start.4
  372.9 75.5 %all-to-all-start.4 = ((bf16[32,24,2048]{2,1,0:T(8,128)(2,1)}), bf16[32,24,2048]{2,1,0:T(8,128)(2,1)}, u32[]{:S(2)}, u32[]{:S(2)}) async-start(bf16[32,24,2048]{2,1,0:T(8,128)(2,1)} %bitcast.88), calls=%async_computation.4 | async-start | bytes 6291456 | tf_op jit(solution)/shard_map/all_to_all | solution.py:135
  448.4 2.5 copy-start.3
where the time goes:
time: 463 us; the launch traced here: 459 us
  waiting for transfers between devices  204 us (44%)
  local copies, waits for them, and re-layouts  78.6 us (17%)
  blocking collectives  75 us (16%)
  matrix products  63.1 us (14%)
  starting transfers between devices  20.5 us (4%)
  other arithmetic  17.2 us (4%)
    all_to_all x1, waiting for transfers between devices, shards(): lax.all_to_all(picked.reshape(head_local, device_count, slot_cap, 3, head...  104 us
    all_to_all x1, blocking collectives, shards(): lax.all_to_all(outgoing, ('seq', 'grp'), split_axis=0, concat_axis=0, til...  75 us
    all_to_all x1, waiting for transfers between devices, shards(): lax.all_to_all(outgoing_back, ('seq', 'grp'), split_axis=0, concat_axis=0...  69.2 us
    gather x3, local copies, waits for them, and re-layouts, shards(): wanted = members[head_range[:, None, None], positions]  52.2 us
    all_to_all x1, waiting for transfers between devices, shards(): lax.all_to_all(for_sending(returning), ('seq', 'grp'), split_axis=1, conc...  30 us
    dot_general x3, matrix products, attend_slots(): jnp.dot(weights, values_all[:row_end], preferred_element_type=jnp.float32)  13 us
    reduce_sum x3, other arithmetic, attend_slots(): totals = jnp.sum(exp_scores, axis=1, keepdims=True)  11.2 us
    dot_general x1, matrix products, expert_mlp(): jnp.dot(hidden, down_w, preferred_element_type=jnp.float32)  11 us
  transfers between devices with their start and end apart: 4, of which 4 were waited for; matrix products, arithmetic and copies ran while one was open for 4% of the time, Pallas kernels for 0%

commit v1 on v0

v1 whole, which is shorter than its diff:
```python
import functools

import jax
import jax.numpy as jnp
from jax import lax
from jax.experimental import pallas as pl
from jax.experimental.pallas import tpu as pltpu
from jax.sharding import PartitionSpec as P

MESH = pl.DeviceIdType.MESH
F32 = jnp.float32
BF16 = jnp.bfloat16


def round_up(value, step):
    return (value + step - 1) // step * step


def select_matrix(code, slots):
    lists, rows = code.shape
    slot_iota = lax.broadcasted_iota(jnp.int32, (slots, rows), 0).astype(F32)
    parts = [
        jnp.where(code[g : g + 1, :] == slot_iota, 1.0, 0.0).astype(BF16) for g in range(lists)
    ]
    return jnp.concatenate(parts, axis=0)


def attention_kernel(
    S, G, H, R, C, dh, scale,
    x_ref, code_ref, bias_ref, out_ref,
    zin, psend, arr, osend, oarr, zback,
    zs_send, zs_recv, ps_send, ps_recv, os_send, os_recv, bs_send, bs_recv,
):
    s = lax.axis_index("seq")
    g = lax.axis_index("grp")

    barrier = pltpu.get_barrier_semaphore()
    for d in range(1, S):
        pl.semaphore_signal(barrier, inc=1, device_id=(lax.rem(s + d, S), g), device_id_type=MESH)
    for d in range(1, G):
        pl.semaphore_signal(barrier, inc=1, device_id=(s, lax.rem(g + d, G)), device_id_type=MESH)
    pl.semaphore_wait(barrier, S + G - 2)

    def z_copy(j, d):
        to = lax.rem(s + d, S)
        return pltpu.make_async_remote_copy(
            src_ref=x_ref.at[to, j], dst_ref=zin.at[j, s],
            send_sem=zs_send.at[j, d], recv_sem=zs_recv.at[j, s],
            device_id=(to, g), device_id_type=MESH,
        )

    def z_own(j):
        return pltpu.make_async_copy(x_ref.at[s, j], zin.at[j, s], zs_recv.at[j, s])

    def z_arrival(j, src):
        return pltpu.make_async_copy(zin.at[j, src], zin.at[j, src], zs_recv.at[j, src])

    def p_copy(j, d):
        to = lax.rem(g + d, G)
        return pltpu.make_async_remote_copy(
            src_ref=psend.at[j, :, to], dst_ref=arr.at[j, :, g],
            send_sem=ps_send.at[j, d], recv_sem=ps_recv.at[j, g],
            device_id=(s, to), device_id_type=MESH,
        )

    def p_own(j):
        return pltpu.make_async_copy(psend.at[j, :, g], arr.at[j, :, g], ps_recv.at[j, g])

    def p_arrival(j, src):
        return pltpu.make_async_copy(arr.at[j, :, src], arr.at[j, :, src], ps_recv.at[j, src])

    def o_copy(j, d):
        to = lax.rem(g + d, G)
        return pltpu.make_async_remote_copy(
            src_ref=osend.at[j, :, to], dst_ref=oarr.at[j, :, g],
            send_sem=os_send.at[j, d], recv_sem=os_recv.at[j, g],
            device_id=(s, to), device_id_type=MESH,
        )

    def o_own(j):
        return pltpu.make_async_copy(osend.at[j, :, g], oarr.at[j, :, g], os_recv.at[j, g])

    def o_arrival(j, src):
        return pltpu.make_async_copy(oarr.at[j, :, src], oarr.at[j, :, src], os_recv.at[j, src])

    def columns(owner, j):
        return pl.ds(pl.multiple_of((owner * H + j) * dh, dh), dh)

    def b_copy(j, d):
        to = lax.rem(s + d, S)
        return pltpu.make_async_remote_copy(
            src_ref=zback.at[j, to], dst_ref=out_ref.at[:, columns(s, j)],
            send_sem=bs_send.at[j, d], recv_sem=bs_recv.at[j, s],
            device_id=(to, g), device_id_type=MESH,
        )

    def b_own(j):
        return pltpu.make_async_copy(
            zback.at[j, s], out_ref.at[:, columns(s, j)], bs_recv.at[j, s]
        )

    def b_arrival(j, src):
        where = out_ref.at[:, columns(src, j)]
        return pltpu.make_async_copy(where, where, bs_recv.at[j, src])

    def z_start(j):
        for d in range(1, S):
            z_copy(j, d).start()
        z_own(j).start()

    z_start(0)
    if H > 1:
        z_start(1)

    def route(j):
        for src in range(S):
            z_arrival(j, src).wait()

        @pl.when(j + 2 < H)
        def _():
            z_start(j + 2)

        for z in range(S):
            sel = select_matrix(code_ref[j, z], C)
            picked = jnp.dot(sel, zin[j, z], preferred_element_type=F32)
            psend[j, z] = picked.astype(BF16).reshape(G, C, 3 * dh)
        for d in range(1, G):
            p_copy(j, d).start()
        p_own(j).start()

    def attend(j):
        for src in range(G):
            p_arrival(j, src).wait()
        n = G * C
        causal = lax.broadcasted_iota(jnp.int32, (n, n), 0) >= lax.broadcasted_iota(
            jnp.int32, (n, n), 1
        )
        for z in range(S):
            q = arr[j, z, :, :, 0:dh].reshape(n, dh)
            scores = []
            for y in range(z + 1):
                k = arr[j, y, :, :, dh : 2 * dh].reshape(n, dh)
                part = lax.dot_general(
                    q, k, (((1,), (1,)), ((), ())), preferred_element_type=F32
                )
                part = part * scale + bias_ref[j, y]
                if y == z:
                    part = jnp.where(causal, part, -1e30)
                scores.append(part)
            top = functools.reduce(
                jnp.maximum, [jnp.max(part, axis=1, keepdims=True) for part in scores]
            )
            total = jnp.zeros((n, 1), F32)
            acc = jnp.zeros((n, dh), F32)
            for y in range(z + 1):
                e = jnp.exp(scores[y] - top)
                total = total + jnp.sum(e, axis=1, keepdims=True)
                v = arr[j, y, :, :, 2 * dh : 3 * dh].reshape(n, dh)
                acc = acc + jnp.dot(e.astype(BF16), v, preferred_element_type=F32)
            osend[j, z] = (acc / total).astype(BF16).reshape(G, C, dh)
        for d in range(1, G):
            o_copy(j, d).start()
        o_own(j).start()

    def give_back(j):
        for src in range(G):
            o_arrival(j, src).wait()
        for z in range(S):
            sel = select_matrix(code_ref[j, z], C)
            rows = lax.dot_general(
                sel, oarr[j, z].reshape(G * C, dh), (((0,), (0,)), ((), ())),
                preferred_element_type=F32,
            )
            zback[j, z] = rows.astype(BF16)
        for d in range(1, S):
            b_copy(j, d).start()
        b_own(j).start()

    @pl.loop(0, H + 2)
    def _(t):
        @pl.when(t < H)
        def _():
            route(t)

        @pl.when((t >= 1) & (t <= H))
        def _():
            attend(t - 1)

        @pl.when(t >= 2)
        def _():
            give_back(t - 2)

    @pl.loop(0, H)
    def _(j):
        for src in range(S):
            b_arrival(j, src).wait()
        for d in range(1, S):
            z_copy(j, d).wait_send()
            b_copy(j, d).wait_send()
        for d in range(1, G):
            p_copy(j, d).wait_send()
            o_copy(j, d).wait_send()


def cluster_attention(x, code, bias, S, G, H, R, C, dh):
    W = 3 * dh
    vmem = pl.BlockSpec(memory_space=pltpu.VMEM)
    pairs = H * S * G * C * G * C * (S + 1) // 2
    return pl.pallas_call(
        functools.partial(attention_kernel, S, G, H, R, C, dh, dh ** (-0.5)),
        out_shape=jax.ShapeDtypeStruct((R, S * H * dh), BF16),
        in_specs=[pl.BlockSpec(memory_space=pl.ANY), vmem, vmem],
        out_specs=vmem,
        scratch_shapes=[
            pltpu.VMEM((H, S, R, W), BF16),
            pltpu.VMEM((H, S, G, C, W), BF16),
            pltpu.VMEM((H, S, G, C, W), BF16),
            pltpu.VMEM((H, S, G, C, dh), BF16),
            pltpu.VMEM((H, S, G, C, dh), BF16),
            pltpu.VMEM((H, S, R, dh), BF16),
            pltpu.SemaphoreType.DMA((H, S)),
            pltpu.SemaphoreType.DMA((H, S)),
            pltpu.SemaphoreType.DMA((H, G)),
            pltpu.SemaphoreType.DMA((H, G)),
            pltpu.SemaphoreType.DMA((H, G)),
            pltpu.SemaphoreType.DMA((H, G)),
            pltpu.SemaphoreType.DMA((H, S)),
            pltpu.SemaphoreType.DMA((H, S)),
        ],
        compiler_params=pltpu.CompilerParams(
            collective_id=0, has_side_effects=True, vmem_limit_bytes=52 * 1024 * 1024
        ),
        cost_estimate=pl.CostEstimate(
            flops=4 * pairs * dh, bytes_accessed=2 * H * S * R * W, transcendentals=pairs
        ),
    )(x, code, bias)


def expert_mlp(rows_in, gate_w, up_w, down_w):
    gate_part = jnp.dot(rows_in, gate_w, preferred_element_type=F32)
    up_part = jnp.dot(rows_in, up_w, preferred_element_type=F32)
    hidden = (jax.nn.silu(gate_part) * up_part).astype(BF16)
    return jnp.dot(hidden, down_w, preferred_element_type=F32).astype(BF16)


def slot_codes(mask):
    rows = mask.shape[-1]
    before = jnp.triu(jnp.ones((rows, rows), BF16), 1)
    ranks = jnp.einsum("...r,rq->...q", mask.astype(BF16), before, preferred_element_type=F32)
    return jnp.where(mask > 0, ranks, -1.0)


def shards(qkv, cluster_lists, w_out, norm_gain, router, expert_lists, w_gate, w_up, w_down):
    R = qkv.shape[0]
    S = lax.axis_size("seq")
    G = lax.axis_size("grp")
    devices = S * G
    H = cluster_lists.shape[0]
    dh = qkv.shape[2] // (H * S)
    my_index = lax.axis_index("seq") * G + lax.axis_index("grp")
    C = round_up(3 * (R // G) // 2, 16)

    x = qkv.reshape(R, 3, S * H, dh).transpose(2, 0, 1, 3).reshape(S, H, R, 3 * dh)
    members = cluster_lists[:, 0, :]
    lanes = 128
    high = (
        (members // lanes)[:, None, :] == jnp.arange(devices * R // lanes, dtype=jnp.int32)[:, None]
    )
    low = (members % lanes)[:, :, None] == jnp.arange(lanes, dtype=jnp.int32)
    mask = jnp.einsum(
        "hip,hpl->hil", high.astype(BF16), low.astype(BF16), preferred_element_type=F32
    ).reshape(H, S, G, R)
    counts = jnp.sum(mask, axis=3)
    slots = jnp.arange(C, dtype=F32)
    bias = jnp.where(slots < counts[..., None], 0.0, -1e30).reshape(H, S, 1, G * C)
    asked = lax.all_to_all(mask.astype(BF16), "grp", split_axis=2, concat_axis=2, tiled=True)
    code = slot_codes(asked)

    attended = cluster_attention(x, code, bias, S, G, H, R, C, dh)
    mixed = jnp.dot(attended, w_out, preferred_element_type=F32).astype(BF16)
    wide = mixed.astype(F32)
    mean_square = jnp.mean(wide * wide, axis=1, keepdims=True)
    normed = (wide * lax.rsqrt(mean_square + 1e-06) * norm_gain.astype(F32)).astype(BF16)
    gates = jax.nn.sigmoid(jnp.dot(normed, router, preferred_element_type=F32))

    E, chosen_len = expert_lists.shape
    cap = 3 * (chosen_len // devices) // 2
    row_iota = jnp.arange(R, dtype=jnp.int32)
    here = expert_lists - my_index * R
    expert_mask = jnp.sum((here[:, :, None] == row_iota).astype(F32), axis=1)
    expert_code = slot_codes(expert_mask)
    match = expert_code[:, None, :] == jnp.arange(cap, dtype=F32)[None, :, None]
    outgoing = jnp.einsum(
        "ecr,rd->ecd", match.astype(BF16), normed, preferred_element_type=F32
    ).astype(BF16)
    incoming = lax.all_to_all(outgoing, ("seq", "grp"), split_axis=0, concat_axis=0, tiled=True)
    back = expert_mlp(
        incoming.reshape(devices * cap, -1), w_gate[0], w_up[0], w_down[0]
    ).reshape(devices, cap, -1)
    results = lax.all_to_all(back, ("seq", "grp"), split_axis=0, concat_axis=0, tiled=True)
    share = jnp.where(match, gates.T[:, None, :], 0.0).astype(BF16)
    combined = jnp.einsum("ecr,ecd->rd", share, results, preferred_element_type=F32)
    return (wide + combined).astype(BF16)


def solution(mesh):
    return jax.shard_map(
        shards,
        mesh=mesh,
        in_specs=(
            P(("seq", "grp"), None, None),
            P("seq", "grp", None),
            P(),
            P(),
            P(),
            P(),
            P(("seq", "grp"), None, None),
            P(("seq", "grp"), None, None),
            P(("seq", "grp"), None, None),
        ),
        out_specs=P(("seq", "grp"), None),
        check_vma=False,
    )
```

time: 463 us -> 322 us (0.70)
  waiting for transfers between devices: 204 us -> 69.7 us
  Pallas kernels: 0 us -> 113 us
  local copies, waits for them, and re-layouts: 78.6 us -> 16 us
  matrix products: 63.1 us -> 30.8 us
  other arithmetic: 17.2 us -> 5.61 us
  starting transfers between devices: 20.5 us -> 8.95 us
    all_to_all x4 -> x2, waiting for transfers between devices: 204 us -> 69.7 us  [the longest x1 69.7 us: shards(): lax.all_to_all(back, ('seq', 'grp'), split_axis=0, concat_axis=0, tiled=T...]
    pallas_call x0 -> x1, Pallas kernels: none -> 113 us  [cluster_attention(): pl.pallas_call(functools.partial(attention_kernel, S, G, H, R, C, dh, dh...]
    gather x4 -> x0, local copies, waits for them, and re-layouts: 58.5 us -> none  [the longest x3 52.2 us: shards(): wanted = members[head_range[:, None, None], positions]]
    dot_general x15 -> x9, matrix products: 63.1 us -> 30.8 us  [the longest x1 11 us: expert_mlp(): return jnp.dot(hidden, down_w, preferred_element_type=F32).astype(BF16)]
    all_to_all x4 -> x2, starting transfers between devices: 20.5 us -> 8.95 us  [the longest x1 5.17 us: shards(): lax.all_to_all(mask.astype(BF16), 'grp', split_axis=2, concat_axis=2, til...]
    reduce_sum x5 -> x2, other arithmetic: 12.7 us -> 2.92 us  [the longest x1 2.82 us: shards(): expert_mask = jnp.sum((here[:, :, None] == row_iota).astype(F32), axis=1)]
    reshape x3, local copies, waits for them, and re-layouts: 11 us -> 5.4 us  [the longest x1 4.68 us: shards(): qkv.reshape(R, 3, S * H, dh).transpose(2, 0, 1, 3).reshape(S, H, R, 3 * dh)]
  transfers between devices with their start and end apart: 4 -> 2, of which waited for: 4 -> 1; matrix products, arithmetic and copies ran while one was open for 4% -> 6% of each run, Pallas kernels for 0% -> 0%
where the time goes in v1:
time: 322 us; the launch traced here: 321 us
  Pallas kernels  113 us (35%)
  blocking collectives  76.8 us (24%)
  waiting for transfers between devices  69.7 us (22%)
  matrix products  30.8 us (10%)
  local copies, waits for them, and re-layouts  16 us (5%)
  starting transfers between devices  8.95 us (3%)
  other arithmetic  5.61 us (2%)
    pallas_call x1, Pallas kernels, cluster_attention(): pl.pallas_call(functools.partial(attention_kernel, S, G, H, R, C, dh, dh...  113 us
    all_to_all x1, blocking collectives, shards(): lax.all_to_all(outgoing, ('seq', 'grp'), split_axis=0, concat_axis=0, til...  76.8 us
    all_to_all x1, waiting for transfers between devices, shards(): lax.all_to_all(back, ('seq', 'grp'), split_axis=0, concat_axis=0, tiled=T...  69.7 us
    dot_general x1, matrix products, expert_mlp(): return jnp.dot(hidden, down_w, preferred_element_type=F32).astype(BF16)  11 us
  transfers between devices with their start and end apart: 2, of which 1 were waited for; matrix products, arithmetic and copies ran while one was open for 6% of the time, Pallas kernels for 0%

profile of v1, /device:TPU:0, one launch (start us, length us, event | category | flops | bytes accessed | tf_op | source)
XLA Modules:
  0.0 321.2 jit_solution(2615710070906128921)
XLA Ops:
  0.0 0.0 copy-start
  0.0 0.9 and_select_fusion
  0.9 0.7 add_select_fusion
  1.7 1.4 fusion.18
  3.2 0.7 copy.57
  3.9 5.2 %all-to-all-start = ((bf16[4,4,8,256]{3,1,0,2:T(4,128)(2,1)}), bf16[4,4,8,256]{3,1,0,2:T(4,128)(2,1)S(1)}, u32[]{:S(2)}, u32[]{:S(2)}) async-start(bf16[4,4,8,256]{3,1,0,2:T(4,128)(2,1)} %copy.57), calls=%async_computation | async-start | bytes 131072 | tf_op jit(solution)/shard_map/all_to_all | solution.py:276
  9.0 0.1 reduce_sum.27
  9.1 0.1 lt.36
  9.2 0.1 lt.37
  9.4 0.1 lt.34
  9.4 0.8 broadcast_subtract_fusion
  10.3 2.8 convert_reduce_fusion
  13.1 0.1 convolution_select_fusion.1
  13.3 0.1 iota_compare_fusion.5
  13.4 4.7 %copy.29 = bf16[256,3,2048]{0,2,1:T(8,128)(2,1)} copy(bf16[256,3,2048]{2,0,1:T(8,128)(2,1)} %param.9) | data formatting | bytes 6291456 | tf_op args[0]
  18.1 3.9 %copy.30 = bf16[16,256,3,128]{1,3,2,0:T(8,128)(2,1)} copy(bf16[16,256,3,128]{1,3,0,2:T(8,128)(2,1)} %bitcast.50) | data formatting | bytes 6291456 | tf_op jit(solution)/shard_map/transpose | solution.py:263
  22.0 0.0 copy-start.3
  22.0 4.7 %copy.34.x_ref = bf16[4,4,256,384]{3,2,1,0:T(8,128)(2,1)} copy(bf16[4,4,256,384]{2,3,1,0:T(8,128)(2,1)} %bitcast.49) | data formatting | bytes 6291456 | tf_op jit(solution)/shard_map/reshape | solution.py:263
  26.7 0.0 copy-done.3
  26.7 0.0 all-to-all-done
  26.7 0.2 convolution_select_fusion.code_ref
  26.9 113.2 %shard_map.91 = bf16[256,2048]{1,0:T(8,128)(2,1)S(1)} custom-call(bf16[4,4,256,384]{3,2,1,0:T(8,128)(2,1)} %copy.34.x_ref, f32[4,4,8,256]{3,2,1,0:T(8,128)S(1)} %convolution_select_fusion.code_ref, f32[4,4,1,384]{3,2,1,0:T(1,128)S(1)} %compare_select_fusion.bias_ref), custom_call_target="tpu_custom_call" | custom-call | flops 3019898880 | bytes 3145728 | tf_op jit(solution)/shard_map/pallas_call | solution.py:209
  140.0 5.8 %fusion.15 = (f32[256]{0:T(256)S(1)}, bf16[256,2048]{1,0:T(8,128)(2,1)S(1)}) fusion(bf16[256,2048]{1,0:T(8,128)(2,1)S(1)} %shard_map.91, bf16[2048,2048]{1,0:T(8,128)(2,1)} %param.11), kind=kOutput, calls=%fused_computation.18 | convolution fusion | flops 2149580544 | bytes 10486784 | tf_op jit(solution)/shard_map/dot_general | solution.py:280
  145.8 0.0 copy-start.2
  145.9 1.1 convolution_convert_fusion.1
  147.0 0.0 copy-start.4
  147.0 76.8 %all_to_all.15 = bf16[32,24,2048]{2,1,0:T(8,128)(2,1)S(1)} all-to-all(bf16[32,24,2048]{2,1,0:T(8,128)(2,1)S(1)} %convolution_convert_fusion.1), channel_id=1, replica_groups=mesh['seq'=4,'grp'=8] {'seq','grp'}, dimensions={0} | all-to-all | bytes 6291456 | tf_op jit(solution)/shard_map/all_to_all | solution.py:296
  223.8 0.0 copy-done.2
  223.8 0.0 copy-start.1
  223.9 1.7 copy-done.1
  225.5 0.0 copy-done.4
  225.5 4.1 %fusion.1 = f32[768,768]{1,0:T(8,128)} fusion(bf16[768,2048]{1,0:T(8,128)(2,1)S(1)} %bitcast.52, bf16[1,2048,768]{2,1,0:T(8,128)(2,1)S(1)} %copy-done.4), kind=kOutput, calls=%fused_computation.5 | convolution fusion | flops 2415919104 | bytes 8650752 | tf_op jit(solution)/shard_map/dot_general | solution.py:241
  229.6 0.0 copy-done
  229.6 11.0 %convolution_convert_fusion = bf16[768,2048]{1,0:T(8,128)(2,1)} fusion(bf16[1,768,2048]{2,1,0:T(8,128)(2,1)S(1)} %copy-done, f32[768,768]{1,0:T(8,128)} %fusion.1, bf16[768,2048]{1,0:T(8,128)(2,1)} %bitcast.53, bf16[1,2048,768]{2,1,0:T(8,128)(2,1)} %param.15), kind=kOutput, calls=%fused_computation.2 | convolution fusion | flops 4836950016 | bytes 14942208 | tf_op jit(solution)/shard_map/dot_general | solution.py:243
  240.6 0.0 copy-start.5
  240.6 3.8 %all-to-all-start.2 = ((bf16[32,24,2048]{2,1,0:T(8,128)(2,1)}), bf16[32,24,2048]{2,1,0:T(8,128)(2,1)}, u32[]{:S(2)}, u32[]{:S(2)}) async-start(bf16[32,24,2048]{2,1,0:T(8,128)(2,1)} %bitcast.51), calls=%async_computation.2 | async-start | bytes 6291456 | tf_op jit(solution)/shard_map/all_to_all | solution.py:300
  244.4 0.0 copy-done.5
  244.4 1.7 fusion.24
  246.1 69.7 %all-to-all-done.2 = bf16[32,24,2048]{2,1,0:T(8,128)(2,1)} async-done(((bf16[32,24,2048]{2,1,0:T(8,128)(2,1)}), bf16[32,24,2048]{2,1,0:T(8,128)(2,1)}, u32[]{:S(2)}, u32[]{:S(2)}) %all-to-all-start.2) | async-done | bytes 3145760 | tf_op jit(solution)/shard_map/all_to_all | solution.py:300
  315.8 5.4 %fusion.12 = bf16[256,2048]{1,0:T(8,128)(2,1)} fusion(bf16[32,24,2048]{2,1,0:T(8,128)(2,1)} %all-to-all-done.2, bf16[256,2048]{1,0:T(8,128)(2,1)} %copy-done.2, bf16[32,256]{1,0:T(8,128)(2,1)S(1)} %fusion.24, f32[32,256]{1,0:T(8,128)S(1)} %convolution_select_fusion.1), kind=kOutput, calls=%fused_computation.15 | convolution fusion | flops 807272448 | bytes 5292032 | tf_op jit(solution)/shard_map/ecr,ecd->rd/dot_general | solution.py:302
  (6 shorter events, 0.1 us)
Async XLA Ops:
  0.0 229.6 %copy-start = (bf16[1,768,2048]{2,1,0:T(8,128)(2,1)S(1)}, bf16[1,768,2048]{2,1,0:T(8,128)(2,1)}, u32[]{:S(2)}) copy-start(bf16[1,768,2048]{2,1,0:T(8,128)(2,1)} %param.17) | copy-start | bytes 9437188
  3.9 22.8 %all-to-all-start = ((bf16[4,4,8,256]{3,1,0,2:T(4,128)(2,1)}), bf16[4,4,8,256]{3,1,0,2:T(4,128)(2,1)S(1)}, u32[]{:S(2)}, u32[]{:S(2)}) async-start(bf16[4,4,8,256]{3,1,0,2:T(4,128)(2,1)} %copy.57), calls=%async_computation | async-start | bytes 131072 | tf_op jit(solution)/shard_map/all_to_all | solution.py:276
  22.0 4.7 %copy-start.3 = (bf16[2048]{0:T(1024)(128)(2,1)S(1)}, bf16[2048]{0:T(1024)(128)(2,1)}, u32[]{:S(2)}) copy-start(bf16[2048]{0:T(1024)(128)(2,1)} %param.12) | copy-start | bytes 12292
  145.8 78.0 %copy-start.2 = (bf16[256,2048]{1,0:T(8,128)(2,1)}, bf16[256,2048]{1,0:T(8,128)(2,1)S(1)}, u32[]{:S(2)}) copy-start(bf16[256,2048]{1,0:T(8,128)(2,1)S(1)} %get-tuple-element.6) | copy-start | bytes 3145732
  147.0 78.5 %copy-start.4 = (bf16[1,2048,768]{2,1,0:T(8,128)(2,1)S(1)}, bf16[1,2048,768]{2,1,0:T(8,128)(2,1)}, u32[]{:S(2)}) copy-start(bf16[1,2048,768]{2,1,0:T(8,128)(2,1)} %param.16) | copy-start | bytes 9437188
  223.8 1.7 copy-start.1
  240.6 3.8 %copy-start.5 = (bf16[2048,32]{0,1:T(8,128)(2,1)S(1)}, bf16[2048,32]{0,1:T(8,128)(2,1)}, u32[]{:S(2)}) copy-start(bf16[2048,32]{0,1:T(8,128)(2,1)} %param.13) | copy-start | bytes 393220
  240.6 75.2 %all-to-all-start.2 = ((bf16[32,24,2048]{2,1,0:T(8,128)(2,1)}), bf16[32,24,2048]{2,1,0:T(8,128)(2,1)}, u32[]{:S(2)}, u32[]{:S(2)}) async-start(bf16[32,24,2048]{2,1,0:T(8,128)(2,1)} %bitcast.51), calls=%async_computation.2 | async-start | bytes 6291456 | tf_op jit(solution)/shard_map/all_to_all | solution.py:300

commit v2 on v1

--- a/solution.py
+++ b/solution.py
@@ -41,16 +41,21 @@
         pl.semaphore_signal(barrier, inc=1, device_id=(s, lax.rem(g + d, G)), device_id_type=MESH)
     pl.semaphore_wait(barrier, S + G - 2)
 
-    def z_copy(j, d):
+    def head_part(owner, j, k):
+        return x_ref.at[:, pl.ds(pl.multiple_of(((k * S + owner) * H + j) * dh, dh), dh)]
+
+    def z_copy(j, d, k):
         to = lax.rem(s + d, S)
         return pltpu.make_async_remote_copy(
-            src_ref=x_ref.at[to, j], dst_ref=zin.at[j, s],
-            send_sem=zs_send.at[j, d], recv_sem=zs_recv.at[j, s],
+            src_ref=head_part(to, j, k), dst_ref=zin.at[j, s, :, k * dh : (k + 1) * dh],
+            send_sem=zs_send.at[j, d, k], recv_sem=zs_recv.at[j, s],
             device_id=(to, g), device_id_type=MESH,
         )
 
-    def z_own(j):
-        return pltpu.make_async_copy(x_ref.at[s, j], zin.at[j, s], zs_recv.at[j, s])
+    def z_own(j, k):
+        return pltpu.make_async_copy(
+            head_part(s, j, k), zin.at[j, s, :, k * dh : (k + 1) * dh], zs_recv.at[j, s]
+        )
 
     def z_arrival(j, src):
         return pltpu.make_async_copy(zin.at[j, src], zin.at[j, src], zs_recv.at[j, src])
@@ -104,9 +109,10 @@
         return pltpu.make_async_copy(where, where, bs_recv.at[j, src])
 
     def z_start(j):
-        for d in range(1, S):
-            z_copy(j, d).start()
-        z_own(j).start()
+        for k in range(3):
+            for d in range(1, S):
+                z_copy(j, d, k).start()
+            z_own(j, k).start()
 
     z_start(0)
     if H > 1:
@@ -195,7 +201,8 @@
         for src in range(S):
             b_arrival(j, src).wait()
         for d in range(1, S):
-            z_copy(j, d).wait_send()
+            for k in range(3):
+                z_copy(j, d, k).wait_send()
             b_copy(j, d).wait_send()
         for d in range(1, G):
             p_copy(j, d).wait_send()
@@ -218,7 +225,7 @@
             pltpu.VMEM((H, S, G, C, dh), BF16),
             pltpu.VMEM((H, S, G, C, dh), BF16),
             pltpu.VMEM((H, S, R, dh), BF16),
-            pltpu.SemaphoreType.DMA((H, S)),
+            pltpu.SemaphoreType.DMA((H, S, 3)),
             pltpu.SemaphoreType.DMA((H, S)),
             pltpu.SemaphoreType.DMA((H, G)),
             pltpu.SemaphoreType.DMA((H, G)),
@@ -236,11 +243,202 @@
     )(x, code, bias)
 
 
-def expert_mlp(rows_in, gate_w, up_w, down_w):
-    gate_part = jnp.dot(rows_in, gate_w, preferred_element_type=F32)
-    up_part = jnp.dot(rows_in, up_w, preferred_element_type=F32)
-    hidden = (jax.nn.silu(gate_part) * up_part).astype(BF16)
-    return jnp.dot(hidden, down_w, preferred_element_type=F32).astype(BF16)
+def expert_kernel(
+    S, G, GC, SC, NQ, Dc,
+    normed_ref, mixed_ref, match_ref, share_ref, perm_ref, wg_hbm, wu_hbm, wd_hbm, out_ref,
+    zsel, zin, psend, parr, rsend, rarr, zout, zfin, wg, wu, wd, gate_acc, up_acc,
+    zs_send, zs_recv, ps_send, ps_recv, rs_send, rs_recv, bs_send, bs_recv, w_sem,
+):
+    s = lax.axis_index("seq")
+    g = lax.axis_index("grp")
+    rows = G * SC
+
+    loads = [
+        pltpu.make_async_copy(wg_hbm, wg, w_sem.at[0]),
+        pltpu.make_async_copy(wu_hbm, wu, w_sem.at[1]),
+        pltpu.make_async_copy(wd_hbm, wd, w_sem.at[2]),
+    ]
+    barrier = pltpu.get_barrier_semaphore()
+    for d in range(1, S):
+        pl.semaphore_signal(barrier, inc=1, device_id=(lax.rem(s + d, S), g), device_id_type=MESH)
+    for d in range(1, G):
+        pl.semaphore_signal(barrier, inc=1, device_id=(s, lax.rem(g + d, G)), device_id_type=MESH)
+
+    def along_seq(source, target, send, recv):
+        def copy(q, d):
+            to = lax.rem(s + d, S)
+            return pltpu.make_async_remote_copy(
+                src_ref=source.at[q, to], dst_ref=target.at[q, s],
+                send_sem=send.at[q, d], recv_sem=recv.at[q, s],
+                device_id=(to, g), device_id_type=MESH,
+            )
+
+        def start(q):
+            for d in range(1, S):
+                copy(q, d).start()
+            pltpu.make_async_copy(source.at[q, s], target.at[q, s], recv.at[q, s]).start()
+
+        def arrive(q):
+            for y in range(S):
+                pltpu.make_async_copy(target.at[q, y], target.at[q, y], recv.at[q, y]).wait()
+
+        def sent(q):
+            for d in range(1, S):
+                copy(q, d).wait_send()
+
+        return start, arrive, sent
+
+    def along_grp(source, target, send, recv):
+        def copy(q, d):
+            to = lax.rem(g + d, G)
+            return pltpu.make_async_remote_copy(
+                src_ref=source.at[q, to], dst_ref=target.at[q, g],
+                send_sem=send.at[q, d], recv_sem=recv.at[q, g],
+                device_id=(s, to), device_id_type=MESH,
+            )
+
+        def start(q):
+            for d in range(1, G):
+                copy(q, d).start()
+            pltpu.make_async_copy(source.at[q, g], target.at[q, g], recv.at[q, g]).start()
+
+        def arrive(q):
+            for y in range(G):
+                pltpu.make_async_copy(target.at[q, y], target.at[q, y], recv.at[q, y]).wait()
+
+        def sent(q):
+            for d in range(1, G):
+                copy(q, d).wait_send()
+
+        return start, arrive, sent
+
+    z_start, z_arrive, z_sent = along_seq(zsel, zin, zs_send, zs_recv)
+    p_start, p_arrive, p_sent = along_grp(psend, parr, ps_send, ps_recv)
+    r_start, r_arrive, r_sent = along_grp(rsend, rarr, rs_send, rs_recv)
+    b_start, b_arrive, b_sent = along_seq(zout, zfin, bs_send, bs_recv)
+
+    def columns(q):
+        return pl.ds(pl.multiple_of(q * Dc, Dc), Dc)
+
+    def select(q):
+        picked = jnp.dot(match_ref[...], normed_ref[:, columns(q)], preferred_element_type=F32)
+        zsel[q] = picked.astype(BF16).reshape(S, GC, Dc)
+
+    select(0)
+    if NQ > 1:
+        select(1)
+    pl.semaphore_wait(barrier, S + G - 2)
+    z_start(0)
+    if NQ > 1:
+        z_start(1)
+    for load in loads:
+        load.start()
+    gate_acc[...] = jnp.zeros_like(gate_acc)
+    up_acc[...] = jnp.zeros_like(up_acc)
+
+    @pl.loop(2, NQ)
+    def _(q):
+        select(q)
+
+    for load in loads:
+        load.wait()
+
+    @pl.loop(0, NQ + 1)
+    def _(t):
+        @pl.when(t < NQ)
+        def _():
+            z_arrive(t)
+
+            @pl.when(t + 2 < NQ)
+            def _():
+                z_start(t + 2)
+
+            moved = jnp.dot(
+                perm_ref[...], zin[t].reshape(rows, Dc), preferred_element_type=F32
+            )
+            psend[t] = moved.astype(BF16).reshape(G, SC, Dc)
+            p_start(t)
+
+        @pl.when(t >= 1)
+        def _():
+            q = t - 1
+            p_arrive(q)
+            taken = parr[q].reshape(rows, Dc)
+            gate_acc[...] += jnp.dot(taken, wg[columns(q), :], preferred_element_type=F32)
+            up_acc[...] += jnp.dot(taken, wu[columns(q), :], preferred_element_type=F32)
+
+    gate = gate_acc[...]
+    hidden = (gate * jax.nn.sigmoid(gate) * up_acc[...]).astype(BF16)
+
+    for q in range(NQ):
+        result = jnp.dot(hidden, wd[:, q * Dc : (q + 1) * Dc], preferred_element_type=F32)
+        rsend[q] = result.astype(BF16).reshape(G, SC, Dc)
+        r_start(q)
+
+    @pl.loop(0, NQ + 2)
+    def _(t):
+        @pl.when(t < NQ)
+        def _():
+            r_arrive(t)
+            moved = lax.dot_general(
+                perm_ref[...], rarr[t].reshape(rows, Dc), (((0,), (0,)), ((), ())),
+                preferred_element_type=F32,
+            )
+            zout[t] = moved.astype(BF16).reshape(S, GC, Dc)
+            b_start(t)
+
+        @pl.when(t >= 2)
+        def _():
+            q = t - 2
+            b_arrive(q)
+            total = jnp.dot(
+                share_ref[...], zfin[q].reshape(rows, Dc), preferred_element_type=F32
+            )
+            out_ref[:, columns(q)] = (mixed_ref[:, columns(q)].astype(F32) + total).astype(BF16)
+
+    @pl.loop(0, NQ)
+    def _(q):
+        z_sent(q)
+        p_sent(q)
+        r_sent(q)
+        b_sent(q)
+
+
+def run_experts(normed, mixed, match, share, perm, wg, wu, wd, S, G, cap):
+    R, D = normed.shape
+    hidden = wg.shape[1]
+    NQ = 8
+    Dc = D // NQ
+    GC, SC = G * cap, S * cap
+    rows = S * GC
+    vmem = pl.BlockSpec(memory_space=pltpu.VMEM)
+    hbm = pl.BlockSpec(memory_space=pl.ANY)
+    by_seq = pltpu.VMEM((NQ, S, GC, Dc), BF16)
+    by_grp = pltpu.VMEM((NQ, G, SC, Dc), BF16)
+    seq_sem = pltpu.SemaphoreType.DMA((NQ, S))
+    grp_sem = pltpu.SemaphoreType.DMA((NQ, G))
+    return pl.pallas_call(
+        functools.partial(expert_kernel, S, G, GC, SC, NQ, Dc),
+        out_shape=jax.ShapeDtypeStruct((R, D), BF16),
+        in_specs=[vmem, vmem, vmem, vmem, vmem, hbm, hbm, hbm],
+        out_specs=vmem,
+        scratch_shapes=[
+            by_seq, by_seq, by_grp, by_grp, by_grp, by_grp, by_seq, by_seq,
+            pltpu.VMEM((D, hidden), BF16),
+            pltpu.VMEM((D, hidden), BF16),
+            pltpu.VMEM((hidden, D), BF16),
+            pltpu.VMEM((rows, hidden), F32),
+            pltpu.VMEM((rows, hidden), F32),
+            seq_sem, seq_sem, grp_sem, grp_sem, grp_sem, grp_sem, seq_sem, seq_sem,
+            pltpu.SemaphoreType.DMA((3,)),
+        ],
+        compiler_params=pltpu.CompilerParams(
+            collective_id=1, has_side_effects=True, vmem_limit_bytes=60 * 1024 * 1024
+        ),
+        cost_estimate=pl.CostEstimate(
+            flops=6 * rows * D * hidden, bytes_accessed=6 * D * hidden, transcendentals=rows * hidden
+        ),
+    )(normed, mixed, match, share, perm, wg, wu, wd)
 
 
 def slot_codes(mask):
@@ -260,7 +458,7 @@
     my_index = lax.axis_index("seq") * G + lax.axis_index("grp")
     C = round_up(3 * (R // G) // 2, 16)
 
-    x = qkv.reshape(R, 3, S * H, dh).transpose(2, 0, 1, 3).reshape(S, H, R, 3 * dh)
+    x = qkv.reshape(R, 3 * S * H * dh)
     members = cluster_lists[:, 0, :]
     lanes = 128
     high = (
@@ -290,17 +488,14 @@
     expert_mask = jnp.sum((here[:, :, None] == row_iota).astype(F32), axis=1)
     expert_code = slot_codes(expert_mask)
     match = expert_code[:, None, :] == jnp.arange(cap, dtype=F32)[None, :, None]
-    outgoing = jnp.einsum(
-        "ecr,rd->ecd", match.astype(BF16), normed, preferred_element_type=F32
-    ).astype(BF16)
-    incoming = lax.all_to_all(outgoing, ("seq", "grp"), split_axis=0, concat_axis=0, tiled=True)
-    back = expert_mlp(
-        incoming.reshape(devices * cap, -1), w_gate[0], w_up[0], w_down[0]
-    ).reshape(devices, cap, -1)
-    results = lax.all_to_all(back, ("seq", "grp"), split_axis=0, concat_axis=0, tiled=True)
-    share = jnp.where(match, gates.T[:, None, :], 0.0).astype(BF16)
-    combined = jnp.einsum("ecr,ecd->rd", share, results, preferred_element_type=F32)
-    return (wide + combined).astype(BF16)
+    share = jnp.where(match, gates.T[:, None, :], 0.0).astype(BF16).reshape(E * cap, R).T
+    match = match.astype(BF16).reshape(E * cap, R)
+    place = jnp.arange(E * cap, dtype=jnp.int32)
+    by_seq = place.reshape(S, G, cap).transpose(1, 0, 2).reshape(-1)
+    perm = (by_seq[:, None] == place[None, :]).astype(BF16)
+    return run_experts(
+        normed, mixed, match, share, perm, w_gate[0], w_up[0], w_down[0], S, G, cap
+    )
 
 
 def solution(mesh):

time: 322 us -> 310 us (0.963)
  Pallas kernels: 113 us -> 276 us
  blocking collectives: 76.8 us -> 0 us
  waiting for transfers between devices: 69.7 us -> 0.01 us
  matrix products: 30.8 us -> 7.96 us
  local copies, waits for them, and re-layouts: 16 us -> 11.4 us
  starting transfers between devices: 8.95 us -> 5.17 us
    pallas_call x0 -> x1, Pallas kernels: none -> 162 us  [run_experts(): pl.pallas_call(functools.partial(expert_kernel, S, G, GC, SC, NQ, Dc), ou...]
    all_to_all x1 -> x0, blocking collectives: 76.8 us -> none  [shards(): lax.all_to_all(outgoing, ('seq', 'grp'), split_axis=0, concat_axis=0, til...]
    all_to_all x1 -> x0, waiting for transfers between devices: 69.7 us -> none  [shards(): lax.all_to_all(back, ('seq', 'grp'), split_axis=0, concat_axis=0, tiled=T...]
    dot_general x4 -> x0, matrix products: 21.6 us -> none  [the longest x1 11 us: expert_mlp(): return jnp.dot(hidden, down_w, preferred_element_type=F32).astype(BF16)]
    transpose x1 -> x0, local copies, waits for them, and re-layouts: 3.89 us -> none  [shards(): qkv.reshape(R, 3, S * H, dh).transpose(2, 0, 1, 3).reshape(S, H, R, 3 * dh)]
    all_to_all x1 -> x0, starting transfers between devices: 3.78 us -> none  [shards(): lax.all_to_all(back, ('seq', 'grp'), split_axis=0, concat_axis=0, tiled=T...]
  transfers between devices with their start and end apart: 2 -> 1, of which waited for: 1 -> 0; matrix products, arithmetic and copies ran while one was open for 6% -> 4% of each run, Pallas kernels for 0% -> 0%
where the time goes in v2:
time: 310 us; the launch traced here: 308 us
  Pallas kernels  276 us (89%)
  local copies, waits for them, and re-layouts  11.4 us (4%)
  matrix products  7.96 us (3%)
  other arithmetic  7.93 us (3%)
  starting transfers between devices  5.17 us (2%)
    pallas_call x1, Pallas kernels, run_experts(): pl.pallas_call(functools.partial(expert_kernel, S, G, GC, SC, NQ, Dc), ou...  162 us
    pallas_call x1, Pallas kernels, cluster_attention(): pl.pallas_call(functools.partial(attention_kernel, S, G, H, R, C, dh, dh...  114 us
  transfers between devices with their start and end apart: 1, of which 0 were waited for; matrix products, arithmetic and copies ran while one was open for 4% of the time, Pallas kernels for 0%

profile of v2, /device:TPU:0, one launch (start us, length us, event | category | flops | bytes accessed | tf_op | source)
XLA Modules:
  0.0 308.2 jit_solution(8710922348014791483)
XLA Ops:
  0.0 0.0 copy-start
  0.0 0.8 add_select_fusion
  0.8 0.8 and_select_fusion
  1.6 1.4 fusion.4
  3.1 0.7 copy.45
  3.7 5.2 %all-to-all-start = ((bf16[4,4,8,256]{3,1,0,2:T(4,128)(2,1)}), bf16[4,4,8,256]{3,1,0,2:T(4,128)(2,1)S(1)}, u32[]{:S(2)}, u32[]{:S(2)}) async-start(bf16[4,4,8,256]{3,1,0,2:T(4,128)(2,1)} %copy.45), calls=%async_computation | async-start | bytes 131072 | tf_op jit(solution)/shard_map/all_to_all | solution.py:474
  8.9 0.1 reduce_sum.27
  9.0 0.1 lt.36
  9.1 0.1 lt.37
  9.2 0.1 lt.34
  9.3 0.8 broadcast_subtract_fusion
  10.2 2.8 convert_reduce_fusion
  13.0 0.1 convolution_select_fusion.1
  13.1 0.1 reshape.115
  13.2 1.3 fusion.perm_ref
  14.6 3.2 %copy.27 = bf16[256,3,2048]{0,2,1:T(8,128)(2,1)S(1)} copy(bf16[256,3,2048]{2,0,1:T(8,128)(2,1)} %param.9) | data formatting | bytes 6291456 | tf_op args[0]
  17.7 0.0 copy-start.3
  17.8 3.1 %copy.31.x_ref = bf16[256,6144]{1,0:T(8,128)(2,1)} copy(bf16[256,6144]{0,1:T(8,128)(2,1)S(1)} %bitcast.28) | data formatting | bytes 6291456 | tf_op jit(solution)/shard_map/reshape | solution.py:461
  20.8 0.0 copy-done.3
  20.9 0.1 eq.87
  20.9 0.3 copy.32
  21.2 0.1 eq.90
  21.3 0.0 all-to-all-done
  21.3 0.2 convolution_select_fusion.code_ref
  21.5 113.8 %shard_map.91 = bf16[256,2048]{1,0:T(8,128)(2,1)S(1)} custom-call(bf16[256,6144]{1,0:T(8,128)(2,1)} %copy.31.x_ref, f32[4,4,8,256]{3,2,1,0:T(8,128)S(1)} %convolution_select_fusion.code_ref, f32[4,4,1,384]{3,2,1,0:T(1,128)S(1)} %compare_select_fusion.bias_ref), custom_call_target="tpu_custom_call" | custom-call | flops 3019898880 | bytes 3145728 | tf_op jit(solution)/shard_map/pallas_call | solution.py:216
  135.3 5.8 %fusion.1 = (f32[256]{0:T(256)S(1)}, bf16[256,2048]{1,0:T(8,128)(2,1)S(1)}) fusion(bf16[256,2048]{1,0:T(8,128)(2,1)S(1)} %shard_map.91, bf16[2048,2048]{1,0:T(8,128)(2,1)} %param.11), kind=kOutput, calls=%fused_computation.7 | convolution fusion | flops 2149580544 | bytes 10486784 | tf_op jit(solution)/shard_map/dot_general | solution.py:478
  141.1 0.0 copy-start.2
  141.1 0.3 fusion.3.normed_ref
  141.4 0.0 copy-done
  141.4 0.0 copy-start.1
  141.4 0.4 fusion.8
  141.9 0.2 copy-done.2
  142.1 0.2 copy.33
  142.3 0.9 fusion.11
  143.2 0.9 copy.34.match_ref
  144.1 0.0 copy-done.1
  144.1 161.8 %shard_map.92 = bf16[256,2048]{1,0:T(8,128)(2,1)} custom-call(bf16[256,2048]{1,0:T(8,128)(2,1)} %copy-done.1, bf16[256,2048]{1,0:T(8,128)(2,1)} %copy-done.2, bf16[768,256]{1,0:T(8,128)(2,1)} %copy.34.match_ref, bf16[256,768]{1,0:T(8,128)(2,1)} %get-tuple-element.5.share_ref, bf16[768,768]{1,0:T(8,128)(2,1)} %fusion.perm_ref, bf16[2048,768]{1,0:T(8,128)(2,1)} %bitcast.32, ...), custom_call_target="tpu_custom_call" | custom-call | flops 7247757312 | bytes 9437184 | tf_op jit(solution)/shard_map/pallas_call | solution.py:420
  305.9 2.3 copy.48
  (10 shorter events, 0.2 us)
Async XLA Ops:
  0.0 141.4 %copy-start = (bf16[2048,32]{0,1:T(8,128)(2,1)S(1)}, bf16[2048,32]{0,1:T(8,128)(2,1)}, u32[]{:S(2)}) copy-start(bf16[2048,32]{0,1:T(8,128)(2,1)} %param.13) | copy-start | bytes 393220
  3.7 17.5 %all-to-all-start = ((bf16[4,4,8,256]{3,1,0,2:T(4,128)(2,1)}), bf16[4,4,8,256]{3,1,0,2:T(4,128)(2,1)S(1)}, u32[]{:S(2)}, u32[]{:S(2)}) async-start(bf16[4,4,8,256]{3,1,0,2:T(4,128)(2,1)} %copy.45), calls=%async_computation | async-start | bytes 131072 | tf_op jit(solution)/shard_map/all_to_all | solution.py:474
  17.7 3.1 %copy-start.3 = (bf16[2048]{0:T(1024)(128)(2,1)S(1)}, bf16[2048]{0:T(1024)(128)(2,1)}, u32[]{:S(2)}) copy-start(bf16[2048]{0:T(1024)(128)(2,1)} %param.12) | copy-start | bytes 12292
  141.1 1.0 copy-start.2
  141.4 2.7 copy-start.1

commit v3 on v2

--- a/solution.py
+++ b/solution.py
@@ -441,6 +441,323 @@
     )(normed, mixed, match, share, perm, wg, wu, wd)
 
 
+def relay_kernel(
+    S, G, GC, SC, NQ, Dc,
+    normed_ref, mixed_ref, match_ref, share_ref, perm_ref, far_ref, router_ref,
+    wg_hbm, wu_hbm, wd_hbm, out_ref,
+    zsel, zin, psend, parr, rsend, rarr, zout, zfin, wg, wu, wd, gate_acc, up_acc,
+    dense, hsel, rel, dout, dfin, logits, far_share,
+    ps_send, ps_recv, rs_send, rs_recv, zs_send, zs_recv, bs_send, bs_recv,
+    d_send, d_recv, h_send, l_send, l_recv, f_send, f_recv, w_sem,
+):
+    s = lax.axis_index("seq")
+    g = lax.axis_index("grp")
+    rows = G * SC
+
+    loads = [
+        pltpu.make_async_copy(wg_hbm, wg, w_sem.at[0]),
+        pltpu.make_async_copy(wu_hbm, wu, w_sem.at[1]),
+        pltpu.make_async_copy(wd_hbm, wd, w_sem.at[2]),
+    ]
+    barrier = pltpu.get_barrier_semaphore()
+    for d in range(1, S):
+        pl.semaphore_signal(barrier, inc=1, device_id=(lax.rem(s + d, S), g), device_id_type=MESH)
+    for d in range(1, G):
+        pl.semaphore_signal(barrier, inc=1, device_id=(s, lax.rem(g + d, G)), device_id_type=MESH)
+
+    side = s // 2
+    spot = s - 2 * side
+    mate = 2 * side + 1 - spot
+    far_first = 2 - 2 * side
+    far_relay = 2 - side
+    relay = (s == 1) | (s == 2)
+
+    def remote(source, target, send, recv, to):
+        return pltpu.make_async_remote_copy(
+            src_ref=source, dst_ref=target, send_sem=send, recv_sem=recv,
+            device_id=(to, g), device_id_type=MESH,
+        )
+
+    def arrived(ref, sem):
+        pltpu.make_async_copy(ref, ref, sem).wait()
+
+    def near_copy(q):
+        return remote(
+            zsel.at[q, 1 - spot], zin.at[q, s], zs_send.at[q], zs_recv.at[q, s], mate
+        )
+
+    def dense_copy(q):
+        return remote(
+            normed_ref.at[:, columns(q)], dense.at[q, spot], d_send.at[q], d_recv.at[q, spot],
+            far_relay,
+        )
+
+    def hop_copy(q, i):
+        y = far_first + i
+        return remote(
+            hsel.at[q, i, 1 - spot], zin.at[q, y], h_send.at[q, i], zs_recv.at[q, y], mate
+        )
+
+    def z_start(q):
+        dense_copy(q).start()
+        near_copy(q).start()
+        pltpu.make_async_copy(zsel.at[q, spot], zin.at[q, s], zs_recv.at[q, s]).start()
+
+    def z_arrive(q):
+        for y in range(S):
+            arrived(zin.at[q, y], zs_recv.at[q, y])
+
+    def relay_rows(q):
+        for i in range(2):
+            y = far_first + i
+            arrived(dense.at[q, i], d_recv.at[q, i])
+            picked = jnp.dot(far_ref[i], dense[q, i], preferred_element_type=F32)
+            hsel[q, i] = picked.astype(BF16).reshape(2, GC, Dc)
+            hop_copy(q, i).start()
+            pltpu.make_async_copy(hsel.at[q, i, spot], zin.at[q, y], zs_recv.at[q, y]).start()
+            logits[i] += lax.dot_general(
+                router_ref[:, columns(q)], dense[q, i], (((1,), (1,)), ((), ())),
+                preferred_element_type=F32,
+            )
+
+    def near_back(q):
+        return remote(
+            zout.at[q, mate], zfin.at[q, spot], bs_send.at[q], bs_recv.at[q, spot], mate
+        )
+
+    def lend_copy(q, i):
+        return remote(
+            zout.at[q, far_first + i], rel.at[q, i], l_send.at[q, i], l_recv.at[q, i], mate
+        )
+
+    def far_copy(q, i):
+        return remote(
+            dout.at[q, i], dfin.at[q], f_send.at[q, i], f_recv.at[q], far_first + i
+        )
+
+    def b_start(q):
+        @pl.when(jnp.logical_not(relay))
+        def _():
+            for i in range(2):
+                lend_copy(q, i).start()
+
+        near_back(q).start()
+        pltpu.make_async_copy(zout.at[q, s], zfin.at[q, spot], bs_recv.at[q, spot]).start()
+
+    def relay_results(q):
+        for i in range(2):
+            arrived(rel.at[q, i], l_recv.at[q, i])
+            mine = lax.dot_general(
+                far_share[i, spot], zout[q, far_first + i], (((0,), (0,)), ((), ())),
+                preferred_element_type=F32,
+            )
+            theirs = lax.dot_general(
+                far_share[i, 1 - spot], rel[q, i], (((0,), (0,)), ((), ())),
+                preferred_element_type=F32,
+            )
+            dout[q, i] = (mine + theirs).astype(BF16)
+            far_copy(q, i).start()
+
+    def b_arrive(q):
+        for i in range(2):
+            arrived(zfin.at[q, i], bs_recv.at[q, i])
+        arrived(dfin.at[q], f_recv.at[q])
+
+    def along_grp(source, target, send, recv):
+        def copy(q, d):
+            to = lax.rem(g + d, G)
+            return pltpu.make_async_remote_copy(
+                src_ref=source.at[q, to], dst_ref=target.at[q, g],
+                send_sem=send.at[q, d], recv_sem=recv.at[q, g],
+                device_id=(s, to), device_id_type=MESH,
+            )
+
+        def start(q):
+            for d in range(1, G):
+                copy(q, d).start()
+            pltpu.make_async_copy(source.at[q, g], target.at[q, g], recv.at[q, g]).start()
+
+        def arrive(q):
+            for y in range(G):
+                pltpu.make_async_copy(target.at[q, y], target.at[q, y], recv.at[q, y]).wait()
+
+        def sent(q):
+            for d in range(1, G):
+                copy(q, d).wait_send()
+
+        return start, arrive, sent
+
+    p_start, p_arrive, p_sent = along_grp(psend, parr, ps_send, ps_recv)
+    r_start, r_arrive, r_sent = along_grp(rsend, rarr, rs_send, rs_recv)
+
+    def columns(q):
+        return pl.ds(pl.multiple_of(q * Dc, Dc), Dc)
+
+    def select(q):
+        picked = jnp.dot(match_ref[...], normed_ref[:, columns(q)], preferred_element_type=F32)
+        zsel[q] = picked.astype(BF16).reshape(2, GC, Dc)
+
+    logits[...] = jnp.zeros_like(logits)
+    select(0)
+    if NQ > 1:
+        select(1)
+    pl.semaphore_wait(barrier, S + G - 2)
+    z_start(0)
+    if NQ > 1:
+        z_start(1)
+    for load in loads:
+        load.start()
+    gate_acc[...] = jnp.zeros_like(gate_acc)
+    up_acc[...] = jnp.zeros_like(up_acc)
+
+    @pl.loop(2, NQ)
+    def _(q):
+        select(q)
+
+        @pl.when(q < 4)
+        def _():
+            z_start(q)
+
+    for load in loads:
+        load.wait()
+
+    @pl.loop(0, NQ + 1)
+    def _(t):
+        @pl.when(t < NQ)
+        def _():
+            @pl.when(relay)
+            def _():
+                relay_rows(t)
+
+            z_arrive(t)
+
+            @pl.when(t + 4 < NQ)
+            def _():
+                z_start(t + 4)
+
+            moved = jnp.dot(
+                perm_ref[...], zin[t].reshape(rows, Dc), preferred_element_type=F32
+            )
+            psend[t] = moved.astype(BF16).reshape(G, SC, Dc)
+            p_start(t)
+
+        @pl.when(t >= 1)
+        def _():
+            q = t - 1
+            p_arrive(q)
+            taken = parr[q].reshape(rows, Dc)
+            gate_acc[...] += jnp.dot(taken, wg[columns(q), :], preferred_element_type=F32)
+            up_acc[...] += jnp.dot(taken, wu[columns(q), :], preferred_element_type=F32)
+
+    gate = gate_acc[...]
+    hidden = (gate * jax.nn.sigmoid(gate) * up_acc[...]).astype(BF16)
+
+    for q in range(NQ):
+        result = jnp.dot(hidden, wd[:, q * Dc : (q + 1) * Dc], preferred_element_type=F32)
+        rsend[q] = result.astype(BF16).reshape(G, SC, Dc)
+        r_start(q)
+
+    @pl.when(relay)
+    def _():
+        for i in range(2):
+            weighted = far_ref[i].astype(F32) * jax.nn.sigmoid(logits[i])
+            far_share[i] = weighted.astype(BF16).reshape(2, GC, weighted.shape[1])
+
+    @pl.loop(0, NQ + 4)
+    def _(t):
+        @pl.when(t < NQ)
+        def _():
+            r_arrive(t)
+            moved = lax.dot_general(
+                perm_ref[...], rarr[t].reshape(rows, Dc), (((0,), (0,)), ((), ())),
+                preferred_element_type=F32,
+            )
+            zout[t] = moved.astype(BF16).reshape(S, GC, Dc)
+            b_start(t)
+
+        @pl.when((t >= 1) & (t <= NQ) & relay)
+        def _():
+            relay_results(t - 1)
+
+        @pl.when(t >= 4)
+        def _():
+            q = t - 4
+            b_arrive(q)
+            total = jnp.dot(
+                share_ref[...], zfin[q].reshape(2 * GC, Dc), preferred_element_type=F32
+            )
+            total = total + dfin[q].astype(F32)
+            out_ref[:, columns(q)] = (mixed_ref[:, columns(q)].astype(F32) + total).astype(BF16)
+
+    @pl.loop(0, NQ)
+    def _(q):
+        p_sent(q)
+        r_sent(q)
+        near_copy(q).wait_send()
+        dense_copy(q).wait_send()
+        near_back(q).wait_send()
+
+        @pl.when(relay)
+        def _():
+            for i in range(2):
+                hop_copy(q, i).wait_send()
+                far_copy(q, i).wait_send()
+
+        @pl.when(jnp.logical_not(relay))
+        def _():
+            for i in range(2):
+                lend_copy(q, i).wait_send()
+
+
+def run_relay(normed, mixed, match, share, perm, far, router, wg, wu, wd, S, G, cap):
+    R, D = normed.shape
+    hidden = wg.shape[1]
+    NQ = 8
+    Dc = D // NQ
+    GC, SC = G * cap, S * cap
+    rows = S * GC
+    vmem = pl.BlockSpec(memory_space=pltpu.VMEM)
+    hbm = pl.BlockSpec(memory_space=pl.ANY)
+    by_seq = pltpu.VMEM((NQ, S, GC, Dc), BF16)
+    pair = pltpu.VMEM((NQ, 2, GC, Dc), BF16)
+    one_sem = pltpu.SemaphoreType.DMA((NQ,))
+    two_sem = pltpu.SemaphoreType.DMA((NQ, 2))
+    by_grp = pltpu.VMEM((NQ, G, SC, Dc), BF16)
+    seq_sem = pltpu.SemaphoreType.DMA((NQ, S))
+    grp_sem = pltpu.SemaphoreType.DMA((NQ, G))
+    return pl.pallas_call(
+        functools.partial(relay_kernel, S, G, GC, SC, NQ, Dc),
+        out_shape=jax.ShapeDtypeStruct((R, D), BF16),
+        in_specs=[vmem] * 7 + [hbm, hbm, hbm],
+        out_specs=vmem,
+        scratch_shapes=[
+            pair, by_seq, by_grp, by_grp, by_grp, by_grp, by_seq, pair,
+            pltpu.VMEM((D, hidden), BF16),
+            pltpu.VMEM((D, hidden), BF16),
+            pltpu.VMEM((hidden, D), BF16),
+            pltpu.VMEM((rows, hidden), F32),
+            pltpu.VMEM((rows, hidden), F32),
+            pltpu.VMEM((NQ, 2, R, Dc), BF16),
+            pltpu.VMEM((NQ, 2, 2, GC, Dc), BF16),
+            pair,
+            pltpu.VMEM((NQ, 2, R, Dc), BF16),
+            pltpu.VMEM((NQ, R, Dc), BF16),
+            pltpu.VMEM((2, 2 * GC, R), F32),
+            pltpu.VMEM((2, 2, GC, R), BF16),
+            grp_sem, grp_sem, grp_sem, grp_sem,
+            one_sem, seq_sem, one_sem, two_sem,
+            one_sem, two_sem, two_sem, two_sem, two_sem, two_sem, one_sem,
+            pltpu.SemaphoreType.DMA((3,)),
+        ],
+        compiler_params=pltpu.CompilerParams(
+            collective_id=2, has_side_effects=True, vmem_limit_bytes=60 * 1024 * 1024
+        ),
+        cost_estimate=pl.CostEstimate(
+            flops=6 * rows * D * hidden, bytes_accessed=6 * D * hidden, transcendentals=rows * hidden
+        ),
+    )(normed, mixed, match, share, perm, far, router, wg, wu, wd)
+
+
 def slot_codes(mask):
     rows = mask.shape[-1]
     before = jnp.triu(jnp.ones((rows, rows), BF16), 1)
@@ -493,6 +810,23 @@
     place = jnp.arange(E * cap, dtype=jnp.int32)
     by_seq = place.reshape(S, G, cap).transpose(1, 0, 2).reshape(-1)
     perm = (by_seq[:, None] == place[None, :]).astype(BF16)
+    if S == 4:
+        side = lax.axis_index("seq") // 2
+        half = E // 2
+        near_lists = lax.dynamic_slice_in_dim(expert_lists, side * half, half, 0)
+        far_block = (2 - 2 * side + jnp.arange(2, dtype=jnp.int32)) * G + lax.axis_index("grp")
+        there = near_lists[None, :, :] - far_block[:, None, None] * R
+        far_mask = jnp.sum((there[..., None] == row_iota).astype(F32), axis=2)
+        far = slot_codes(far_mask)[:, :, None, :] == jnp.arange(cap, dtype=F32)[:, None]
+        far = far.astype(BF16).reshape(2, half * cap, R)
+        near_router = lax.dynamic_slice_in_dim(router.T, side * half, half, 0)
+        near_router = jnp.repeat(near_router, cap, axis=0)
+        near_match = lax.dynamic_slice_in_dim(match, side * half * cap, half * cap, 0)
+        near_share = lax.dynamic_slice_in_dim(share, side * half * cap, half * cap, 1)
+        return run_relay(
+            normed, mixed, near_match, near_share, perm, far, near_router,
+            w_gate[0], w_up[0], w_down[0], S, G, cap,
+        )
     return run_experts(
         normed, mixed, match, share, perm, w_gate[0], w_up[0], w_down[0], S, G, cap
     )

time: 310 us -> 293 us (0.945)
  Pallas kernels: 276 us -> 252 us
  other arithmetic: 7.93 us -> 11.6 us
    pallas_call x1, Pallas kernels: 162 us -> 138 us  [run_relay(): pl.pallas_call(functools.partial(relay_kernel, S, G, GC, SC, NQ, Dc), out...]
    unnamed x11 -> x20, local copies, waits for them, and re-layouts: 5.65 us -> 6.41 us
  transfers between devices with their start and end apart: 1 -> 1, of which waited for: 0 -> 0; matrix products, arithmetic and copies ran while one was open for 4% -> 6% of each run, Pallas kernels for 0% -> 0%
where the time goes in v3:
time: 293 us; the launch traced here: 292 us
  Pallas kernels  252 us (86%)
  local copies, waits for them, and re-layouts  14 us (5%)
  other arithmetic  11.6 us (4%)
  matrix products  9.02 us (3%)
  starting transfers between devices  5.17 us (2%)
    pallas_call x1, Pallas kernels, run_relay(): pl.pallas_call(functools.partial(relay_kernel, S, G, GC, SC, NQ, Dc), out...  138 us
    pallas_call x1, Pallas kernels, cluster_attention(): pl.pallas_call(functools.partial(attention_kernel, S, G, H, R, C, dh, dh...  114 us
    unnamed x20, local copies, waits for them, and re-layouts  6.41 us
  transfers between devices with their start and end apart: 1, of which 0 were waited for; matrix products, arithmetic and copies ran while one was open for 6% of the time, Pallas kernels for 0%

profile of v3, /device:TPU:0, one launch (start us, length us, event | category | flops | bytes accessed | tf_op | source)
XLA Modules:
  0.0 291.7 jit_solution(3689727192857627886)
XLA Ops:
  0.0 0.0 copy-start
  0.0 0.0 copy-start.6
  0.0 0.8 and_select_fusion
  0.8 0.7 add_select_fusion
  1.6 1.4 fusion.4
  3.1 0.7 copy.46
  3.7 5.2 %all-to-all-start = ((bf16[4,4,8,256]{3,1,0,2:T(4,128)(2,1)}), bf16[4,4,8,256]{3,1,0,2:T(4,128)(2,1)}, u32[]{:S(2)}, u32[]{:S(2)}) async-start(bf16[4,4,8,256]{3,1,0,2:T(4,128)(2,1)} %copy.46), calls=%async_computation | async-start | bytes 131072 | tf_op jit(solution)/shard_map/all_to_all | solution.py:791
  8.9 0.1 reduce_sum.36
  9.0 0.1 lt.44
  9.1 0.1 lt.45
  9.3 0.1 lt.42
  9.3 0.8 broadcast_subtract_fusion.1
  10.2 2.8 convert_reduce_fusion.1
  13.0 0.1 convolution_select_fusion.2
  13.2 0.1 eq.120
  13.2 0.3 copy.32
  13.5 0.1 eq.123
  13.6 0.0 copy-done.6
  13.6 0.0 copy-done
  13.7 0.6 dynamic-slice_bitcast_fusion
  14.3 0.1 broadcast_subtract_fusion
  14.4 2.8 convert_reduce_fusion
  17.2 0.1 convolution_select_fusion.1
  17.3 0.1 reshape.132
  17.5 1.3 fusion.perm_ref
  18.8 0.1 broadcast_compare_fusion
  18.9 0.0 copy-start.3
  18.9 0.7 copy-done.3
  19.6 3.2 %copy.27 = bf16[256,3,2048]{0,2,1:T(8,128)(2,1)S(1)} copy(bf16[256,3,2048]{2,0,1:T(8,128)(2,1)} %param.9) | data formatting | bytes 6291456 | tf_op args[0]
  22.8 0.0 copy-start.7
  22.8 3.1 %copy.31.x_ref = bf16[256,6144]{1,0:T(8,128)(2,1)} copy(bf16[256,6144]{0,1:T(8,128)(2,1)S(1)} %bitcast.38) | data formatting | bytes 6291456 | tf_op jit(solution)/shard_map/reshape | solution.py:778
  25.9 0.0 copy-done.7
  25.9 0.8 copy.34.match_ref
  26.7 0.1 eq.135
  26.8 0.9 fusion.10.far_ref
  27.7 0.0 all-to-all-done
  27.7 1.1 convolution_select_fusion.code_ref
  28.8 114.0 %shard_map.91 = bf16[256,2048]{1,0:T(8,128)(2,1)S(1)} custom-call(bf16[256,6144]{1,0:T(8,128)(2,1)} %copy.31.x_ref, f32[4,4,8,256]{3,2,1,0:T(8,128)S(1)} %convolution_select_fusion.code_ref, f32[4,4,1,384]{3,2,1,0:T(1,128)S(1)} %compare_select_fusion.bias_ref), custom_call_target="tpu_custom_call" | custom-call | flops 3019898880 | bytes 3145728 | tf_op jit(solution)/shard_map/pallas_call | solution.py:216
  142.8 5.8 %fusion.1 = (f32[256]{0:T(256)S(1)}, bf16[256,2048]{1,0:T(8,128)(2,1)S(1)}) fusion(bf16[256,2048]{1,0:T(8,128)(2,1)S(1)} %shard_map.91, bf16[2048,2048]{1,0:T(8,128)(2,1)} %param.11), kind=kOutput, calls=%fused_computation.9 | convolution fusion | flops 2149580544 | bytes 10486784 | tf_op jit(solution)/shard_map/dot_general | solution.py:795
  148.6 0.0 copy-start.2
  148.6 0.0 copy-start.4
  148.6 0.0 copy-start.5
  148.6 0.3 fusion.3.normed_ref
  149.0 0.0 copy-start.1
  149.0 0.4 fusion.8
  149.5 0.2 copy.38
  149.7 0.1 copy-done.4
  149.7 0.7 fusion.16.share_ref
  150.5 0.0 copy-done.5
  150.5 1.3 broadcast_in_dim.70
  151.8 0.0 copy-done.2
  151.8 0.0 copy-done.1
  151.8 137.6 %shard_map.92 = bf16[256,2048]{1,0:T(8,128)(2,1)} custom-call(bf16[256,2048]{1,0:T(8,128)(2,1)} %copy-done.1, bf16[256,2048]{1,0:T(8,128)(2,1)} %copy-done.2, bf16[384,256]{1,0:T(8,128)(2,1)} %copy.34.match_ref, bf16[256,384]{1,0:T(8,128)(2,1)} %fusion.16.share_ref, bf16[768,768]{1,0:T(8,128)(2,1)} %fusion.perm_ref, bf16[2,384,256]{2,1,0:T(8,128)(2,1)} %fusion.10.far_ref, ...), custom_call_target="tpu_custom_call" | custom-call | flops 7247757312 | bytes 9437184 | tf_op jit(solution)/shard_map/pallas_call | solution.py:728
  289.4 2.3 copy.49
  (14 shorter events, 0.2 us)
Async XLA Ops:
  0.0 13.6 %copy-start = (bf16[2048,32]{0,1:T(8,128)(2,1)S(1)}, bf16[2048,32]{0,1:T(8,128)(2,1)}, u32[]{:S(2)}) copy-start(bf16[2048,32]{0,1:T(8,128)(2,1)} %param.13) | copy-start | bytes 393220
  0.0 13.6 %copy-start.6 = (s32[32,512]{1,0:T(8,128)S(1)}, s32[32,512]{1,0:T(8,128)}, u32[]{:S(2)}) copy-start(s32[32,512]{1,0:T(8,128)} %param.14) | copy-start | bytes 196612
  3.7 24.0 %all-to-all-start = ((bf16[4,4,8,256]{3,1,0,2:T(4,128)(2,1)}), bf16[4,4,8,256]{3,1,0,2:T(4,128)(2,1)}, u32[]{:S(2)}, u32[]{:S(2)}) async-start(bf16[4,4,8,256]{3,1,0,2:T(4,128)(2,1)} %copy.46), calls=%async_computation | async-start | bytes 131072 | tf_op jit(solution)/shard_map/all_to_all | solution.py:791
  18.9 0.7 copy-start.3
  22.8 3.1 %copy-start.7 = (bf16[2048]{0:T(1024)(128)(2,1)S(1)}, bf16[2048]{0:T(1024)(128)(2,1)}, u32[]{:S(2)}) copy-start(bf16[2048]{0:T(1024)(128)(2,1)} %param.12) | copy-start | bytes 12292
  148.6 3.2 %copy-start.2 = (bf16[256,2048]{1,0:T(8,128)(2,1)}, bf16[256,2048]{1,0:T(8,128)(2,1)S(1)}, u32[]{:S(2)}) copy-start(bf16[256,2048]{1,0:T(8,128)(2,1)S(1)} %get-tuple-element.6.mixed_ref) | copy-start | bytes 3145732
  148.6 1.1 copy-start.4
  148.6 1.8 copy-start.5
  149.0 2.8 copy-start.1
